TPU v7x, 256 devices: a whole 4x4x8 slice. The times are simulated.
256 devices in a mesh: seq: 32 (over y, x, core), dp: 8 (over z).
Axes of the slice: x: 4, y: 4, z: 8, core: 2. Of those that a mesh axis runs over, the one named last changes fastest.
Arguments:
- tokens: bfloat16 [8, 8192, 2048], P('dp', 'seq'), may hold values from -6 to 6
- w_qkv: bfloat16 [2048, 3, 1024], P('seq'), may hold values from -0.125 to 0.125
- weight_table: float32 [16, 8], replicated, may hold values from 0.3 to 3
- weight_index: int32 [8, 64, 6], P('dp', 'seq'), may hold values from 0 to 15
- cotangent: bfloat16 [8, 8192, 1024], P('dp', 'seq'), may hold values from -6 to 6
Outputs:
- attn_out: bfloat16 [8, 8192, 1024], P('dp', 'seq')
- grad_w: float32 [2048, 3, 1024], P('seq')
All inputs are finite; a program needn't handle non-finite values.
Results may differ from a plain program's by a relative error of at most 0.02.
Values may be sent and summed in bfloat16 or wider, within the bound.
No kernel may reach another device: no remote copies, remote signals or barrier semaphores. Data moves between devices by JAX's collectives and lax.ppermute only.
A program may use at most 128 MiB of HBM per device.

v0:
```python
import math
import jax
import jax.numpy as jnp
from jax import lax
from jax.sharding import PartitionSpec as P


def swapped(value, axis, bit):
    mask = 2**bit
    pairs = [(source, source ^ mask) for source in range(lax.axis_size(axis))]
    return lax.ppermute(value, axis, pairs)


def level_factors(weight_table, weight_index, block_len):
    table_rows = weight_table.shape[0]
    chosen = weight_index[0]
    onehot = (chosen[:, :, None] == jnp.arange(table_rows, dtype=jnp.int32)[None, None, :]).astype(
        jnp.float32
    )
    per_block = jnp.einsum("blw,wh->blh", onehot, weight_table, precision=lax.Precision.HIGHEST)
    groups = chosen.shape[0]
    spread = jnp.broadcast_to(
        per_block[:, None], (groups, block_len // groups, chosen.shape[1], weight_table.shape[1])
    )
    return spread.reshape(block_len, chosen.shape[1], weight_table.shape[1])


def make_adder(inputs, columns, shard_rows):
    flat_rows = shard_rows.reshape(shard_rows.shape[0], columns)
    return jnp.dot(inputs, flat_rows, preferred_element_type=jnp.float32)


def climb(keys_bf, values_bf, levels):
    running = jnp.einsum("shd,she->hde", keys_bf, values_bf, preferred_element_type=jnp.float32)
    partners = []
    for bit_pos in range(levels):
        partner = swapped(running.astype(jnp.bfloat16), "seq", bit_pos).astype(running.dtype)
        partners.append(partner)
        running = running + partner
    return partners


def descend(level_grads, levels, device):
    carried = [level_grads[:, bit_pos] for bit_pos in range(levels)]
    gathered = jnp.zeros_like(level_grads[:, 0])
    for bit_pos in range(levels):
        outgoing = jnp.stack(carried[bit_pos:], axis=1)
        incoming = swapped(outgoing.astype(jnp.bfloat16), "seq", bit_pos).astype(outgoing.dtype)
        keeping = (1 - device // 2**bit_pos % 2).astype(jnp.float32)
        gathered = gathered + keeping * incoming[:, 0]
        for upper in range(bit_pos + 1, levels):
            carried[upper] = carried[upper] + incoming[:, upper - bit_pos]
    return gathered


def per_device(tokens, w_qkv, weight_table, weight_index, cotangent):
    inputs = tokens[0]
    block_len = inputs.shape[0]
    inner_width = w_qkv.shape[2]
    head_count = weight_table.shape[1]
    head_dim = inner_width // head_count
    levels = lax.axis_size("seq").bit_length() - 1
    device = lax.axis_index("seq")
    projected = make_adder(
        inputs, 3 * inner_width, lax.all_gather(w_qkv, "seq", axis=0, tiled=True)
    )
    projected = projected.astype(jnp.bfloat16).reshape(block_len, 3, head_count, head_dim)
    queries = projected[:, 0]
    keys_bf = projected[:, 1]
    values_bf = projected[:, 2]
    partners = climb(keys_bf, values_bf, levels)
    level_states = jnp.stack(partners, axis=2).astype(jnp.bfloat16)
    powers = 2 ** jnp.arange(levels, dtype=jnp.int32)
    bit_flags = (device // powers % 2).astype(jnp.float32)
    halves = 2.0 ** jnp.arange(levels, dtype=jnp.float32)
    scale_level = bit_flags / jnp.sqrt(head_dim * halves * block_len)
    weights_tok = level_factors(weight_table, weight_index, block_len)
    level_coef = jnp.transpose(weights_tok[:, 1 : levels + 1, :], (0, 2, 1)) * scale_level
    local_scale = weights_tok[:, 0, :] / math.sqrt(head_dim * block_len)
    row_scale = jnp.transpose(local_scale)[:, :, None]
    causal = jnp.arange(block_len)[:, None] >= jnp.arange(block_len)[None, :]
    raw_scores = jnp.einsum("thd,shd->hts", queries, keys_bf, preferred_element_type=jnp.float32)
    scores = jnp.where(causal[None], raw_scores * row_scale, 0.0).astype(jnp.bfloat16)
    local_out = jnp.einsum("hts,she->the", scores, values_bf, preferred_element_type=jnp.float32)
    far_terms = jnp.einsum(
        "thd,hdle->thle", queries, level_states, preferred_element_type=jnp.float32
    )
    attended = local_out + jnp.sum(far_terms * level_coef[..., None], axis=2)
    attn_out = attended.astype(jnp.bfloat16).reshape(1, block_len, inner_width)
    upstream = cotangent[0].reshape(block_len, head_count, head_dim)
    raw_grads = jnp.einsum("the,she->hts", upstream, values_bf, preferred_element_type=jnp.float32)
    dscores = jnp.where(causal[None], raw_grads * row_scale, 0.0).astype(jnp.bfloat16)
    far_grads = jnp.einsum(
        "the,hdle->thld", upstream, level_states, preferred_element_type=jnp.float32
    )
    grad_q = jnp.einsum("hts,shd->thd", dscores, keys_bf, preferred_element_type=jnp.float32)
    grad_q = grad_q + jnp.sum(far_grads * level_coef[..., None], axis=2)
    grad_k = jnp.einsum("hts,thd->shd", dscores, queries, preferred_element_type=jnp.float32)
    grad_v = jnp.einsum("hts,the->she", scores, upstream, preferred_element_type=jnp.float32)
    scaled = (queries.astype(jnp.float32)[:, :, None, :] * level_coef[..., None]).astype(
        jnp.bfloat16
    )
    level_grads = jnp.einsum("thld,the->hlde", scaled, upstream, preferred_element_type=jnp.float32)
    state_grads = descend(level_grads, levels, device).astype(jnp.bfloat16)
    grad_k = grad_k + jnp.einsum(
        "she,hde->shd", values_bf, state_grads, preferred_element_type=jnp.float32
    )
    grad_v = grad_v + jnp.einsum(
        "shd,hde->she", keys_bf, state_grads, preferred_element_type=jnp.float32
    )
    qkv_grads = (
        jnp.stack([grad_q, grad_k, grad_v], axis=1)
        .astype(jnp.bfloat16)
        .reshape(block_len, 3 * inner_width)
    )
    shard_rows = w_qkv.shape[0]
    partial_value = jnp.einsum("tr,tc->rc", inputs, qkv_grads, preferred_element_type=jnp.float32)
    seq_sum = lax.psum_scatter(
        partial_value.reshape(lax.axis_size("seq") * shard_rows, 3, inner_width).astype(
            jnp.bfloat16
        ),
        "seq",
        scatter_dimension=0,
        tiled=True,
    )
    grad_w = lax.psum(seq_sum, "dp").astype(jnp.float32)
    return (attn_out, grad_w)


def solution(mesh):
    return jax.shard_map(
        per_device,
        mesh=mesh,
        in_specs=(
            P("dp", "seq", None),
            P("seq", None, None),
            P(),
            P("dp", "seq", None),
            P("dp", "seq", None),
        ),
        out_specs=(P("dp", "seq", None), P("seq", None, None)),
        check_vma=False,
    )
```

profile of v0, /device:TPU:2, one launch (start us, length us, event | category | flops | bytes accessed | tf_op | source)
XLA Modules:
  0.0 420.0 jit_solution(265844752788603229)
XLA Ops:
  9.2 1.1 copy.96
  10.4 71.2 %all-gather.2.cloned.1.call-done = bf16[2048,3,1024]{2,0,1:T(8,128)(2,1)} async-done(((bf16[64,3,1024]{2,0,1:T(8,128)(2,1)}), bf16[2048,3,1024]{2,0,1:T(8,128)(2,1)}) %all-gather.2.cloned.1.call-update) | async-done | bytes 12582928 | tf_op jit(solution)/shard_map/all_gather | solution.py:65
  81.5 17.0 %copy.52 = bf16[2048,3,1024]{0,2,1:T(8,128)(2,1)} copy(bf16[2048,3,1024]{2,0,1:T(8,128)(2,1)} %all-gather.2.cloned.1.call-done) | data formatting | bytes 25165824 | tf_op jit(solution)/shard_map/all_gather | solution.py:65
  98.5 8.0 %fusion.6 = bf16[32,8,24,128]{3,1,2,0:T(8,128)(2,1)S(1)} fusion(bf16[2048,3072]{0,1:T(8,128)(2,1)} %bitcast.131, bf16[1,256,2048]{2,1,0:T(8,128)(2,1)S(1)} %copy-done), kind=kOutput, calls=%fused_computation.14 | convolution fusion | flops 3222011904 | bytes 15204352 | tf_op jit(solution)/shard_map/dot_general | solution.py:30
  108.9 2.5 copy.68
  111.5 3.9 fusion.67
  116.8 1.3 copy.92
  119.7 1.8 convert_element_type.144
  123.6 1.5 collective-permute-start.1
  125.5 27.9 %collective-permute-done.1 = bf16[8,128,128]{2,1,0:T(8,128)(2,1)S(1)} collective-permute-done((bf16[8,128,128]{2,1,0:T(8,128)(2,1)S(1)}, bf16[8,128,128]{2,1,0:T(8,128)(2,1)S(1)}, u32[]{:S(2)}, u32[]{:S(2)}) %collective-permute-start.1) | collective-permute-done | bytes 262176 | tf_op jit(solution)/shard_map/ppermute | solution.py:11
  153.4 2.4 collective-permute-start.2
  156.5 1.5 collective-permute-start.7
  158.0 6.4 %collective-permute-done.2 = bf16[8,128,128]{2,1,0:T(8,128)(2,1)S(1)} collective-permute-done((bf16[8,128,128]{2,1,0:T(8,128)(2,1)S(1)}, bf16[8,128,128]{2,1,0:T(8,128)(2,1)S(1)}, u32[]{:S(2)}, u32[]{:S(2)}) %collective-permute-start.2) | collective-permute-done | bytes 262176 | tf_op jit(solution)/shard_map/ppermute | solution.py:11
  164.9 6.8 %collective-permute-done.3 = bf16[8,128,128]{2,1,0:T(8,128)(2,1)S(1)} collective-permute-done((bf16[8,128,128]{2,1,0:T(8,128)(2,1)S(1)}, bf16[8,128,128]{2,1,0:T(8,128)(2,1)S(1)}, u32[]{:S(2)}, u32[]{:S(2)}) %collective-permute-start.3) | collective-permute-done | bytes 262176 | tf_op jit(solution)/shard_map/ppermute | solution.py:11
  172.9 6.8 %collective-permute-done.7 = bf16[8,3,128,128]{3,2,1,0:T(8,128)(2,1)S(1)} collective-permute-done((bf16[8,3,128,128]{3,2,1,0:T(8,128)(2,1)S(1)}, bf16[8,3,128,128]{3,2,1,0:T(8,128)(2,1)S(1)}, u32[]{:S(2)}, u32[]{:S(2)}) %collective-permute-start.7) | collective-permute-done | bytes 786464 | tf_op jit(solution)/shard_map/ppermute | solution.py:11
  180.6 12.1 %collective-permute-done.8 = bf16[8,2,128,128]{3,2,1,0:T(8,128)(2,1)S(1)} collective-permute-done((bf16[8,2,128,128]{3,2,1,0:T(8,128)(2,1)S(1)}, bf16[8,2,128,128]{3,2,1,0:T(8,128)(2,1)S(1)}, u32[]{:S(2)}, u32[]{:S(2)}) %collective-permute-start.8) | collective-permute-done | bytes 524320 | tf_op jit(solution)/shard_map/ppermute | solution.py:11
  192.9 1.9 collective-permute-start.9
  196.2 4.7 %collective-permute-done.9 = bf16[8,1,128,128]{3,2,1,0:T(8,128)(2,1)S(1)} collective-permute-done((bf16[8,1,128,128]{3,2,1,0:T(8,128)(2,1)S(1)}, bf16[8,1,128,128]{3,2,1,0:T(8,128)(2,1)S(1)}, u32[]{:S(2)}, u32[]{:S(2)}) %collective-permute-start.9) | collective-permute-done | bytes 262176 | tf_op jit(solution)/shard_map/ppermute | solution.py:11
  201.9 6.3 %convolution_convert_fusion = bf16[3072,2048]{1,0:T(8,128)(2,1)} fusion(bf16[256,3072]{0,1:T(8,128)(2,1)S(1)} %bitcast.132, bf16[1,256,2048]{2,1,0:T(8,128)(2,1)S(1)} %copy-done), kind=kOutput, calls=%fused_computation | convolution fusion | flops 3227516928 | bytes 15204352 | tf_op jit(solution)/shard_map/tr,tc->rc/dot_general | solution.py:117
  208.2 16.6 %copy.73 = bf16[2048,3,1024]{2,0,1:T(8,128)(2,1)} copy(bf16[2048,3,1024]{0,2,1:T(8,128)(2,1)} %bitcast.130) | data formatting | bytes 25165824 | tf_op jit(solution)/shard_map/convert_element_type | solution.py:119
  225.0 111.3 %reduce-scatter.2.cloned.1.call-done = bf16[64,3,1024]{2,0,1:T(8,128)(2,1)} async-done(((bf16[2048,3,1024]{2,0,1:T(8,128)(2,1)}), bf16[64,3,1024]{2,0,1:T(8,128)(2,1)}) %reduce-scatter.2.cloned.1.call-update) | async-done | bytes 393232 | tf_op jit(solution)/shard_map/reduce_scatter | solution.py:118
  336.3 2.4 fusion.1
  340.2 71.2 %all-reduce.2.cloned.1.call-done = bf16[64,3,1024]{2,0,1:T(8,128)(2,1)} async-done(((bf16[64,3,1024]{2,0,1:T(8,128)(2,1)}), bf16[64,3,1024]{2,0,1:T(8,128)(2,1)}) %all-reduce.2.cloned.1.call-update) | async-done | bytes 393232 | tf_op jit(solution)/shard_map/psum | solution.py:126
  411.5 2.0 convert_element_type.159
  (72 shorter events, 17.1 us)
Async XLA Ops:
  7.2 91.3 %copy-start = (bf16[1,256,2048]{2,1,0:T(8,128)(2,1)S(1)}, bf16[1,256,2048]{2,1,0:T(8,128)(2,1)}, u32[]{:S(2)}) copy-start(bf16[1,256,2048]{2,1,0:T(8,128)(2,1)} %param.5) | copy-start | bytes 3145732
  7.2 74.3 %all-gather.2.cloned.1.call-start = ((), (), s32[]{:S(2)}) async-start(), calls=%async_computation.1 | async-start | bytes 12976128 | tf_op jit(solution)/shard_map/all_gather | solution.py:65
  7.9 328.4 %reduce-scatter.2.cloned.1.call-start = ((), (), s32[]{:S(2)}) async-start(), calls=%async_computation.2 | async-start | bytes 12976128 | tf_op jit(solution)/shard_map/reduce_scatter | solution.py:118
  115.4 4.3 %collective-permute-start.5 = (bf16[8,5,128,128]{3,2,1,0:T(8,128)(2,1)}, bf16[8,5,128,128]{3,2,1,0:T(8,128)(2,1)}, u32[]{:S(2)}, u32[]{:S(2)}) collective-permute-start(bf16[8,5,128,128]{3,2,1,0:T(8,128)(2,1)} %get-tuple-element.23), channel_id=1, source_target_pairs={{0,8},{8,0},{16,24},{24,16},{32,40},{40,32},{48,56},{56,48},{64,72... | collective-permute-start | bytes 3932168 | tf_op jit(solution)/shard_map/ppermute | solution.py:11
  118.2 1.2 copy-start.4
  118.5 5.0 %collective-permute-start = (bf16[8,128,128]{2,1,0:T(8,128)(2,1)S(1)}, bf16[8,128,128]{2,1,0:T(8,128)(2,1)S(1)}, u32[]{:S(2)}, u32[]{:S(2)}) collective-permute-start(bf16[8,128,128]{2,1,0:T(8,128)(2,1)S(1)} %get-tuple-element.21), channel_id=1, source_target_pairs={{0,8},{8,0},{16,24},{24,16},{32,40},{40,32},{48,56},{56,48},{64,72... | collective-permute-start | bytes 786440 | tf_op jit(solution)/shard_map/ppermute | solution.py:11
  119.4 2.1 copy-start.2
  119.7 2.2 copy-start.1
  122.3 33.5 %collective-permute-start.6 = (bf16[8,4,128,128]{3,2,1,0:T(8,128)(2,1)S(1)}, bf16[8,4,128,128]{3,2,1,0:T(8,128)(2,1)S(1)}, u32[]{:S(2)}, u32[]{:S(2)}) collective-permute-start(bf16[8,4,128,128]{3,2,1,0:T(8,128)(2,1)S(1)} %pad_maximum_fusion.1), channel_id=1, source_target_pairs={{0,16},{8,24},{16,0},{24,8},{32,48},{40,56},{48,32},{56,40},{64,80... | collective-permute-start | bytes 3145736 | tf_op jit(solution)/shard_map/ppermute | solution.py:11
  123.6 29.8 %collective-permute-start.1 = (bf16[8,128,128]{2,1,0:T(8,128)(2,1)S(1)}, bf16[8,128,128]{2,1,0:T(8,128)(2,1)S(1)}, u32[]{:S(2)}, u32[]{:S(2)}) collective-permute-start(bf16[8,128,128]{2,1,0:T(8,128)(2,1)S(1)} %fusion.41), channel_id=1, source_target_pairs={{0,16},{8,24},{16,0},{24,8},{32,48},{40,56},{48,32},{56,40},{64,80... | collective-permute-start | bytes 786440 | tf_op jit(solution)/shard_map/ppermute | solution.py:11
  153.4 11.0 %collective-permute-start.2 = (bf16[8,128,128]{2,1,0:T(8,128)(2,1)S(1)}, bf16[8,128,128]{2,1,0:T(8,128)(2,1)S(1)}, u32[]{:S(2)}, u32[]{:S(2)}) collective-permute-start(bf16[8,128,128]{2,1,0:T(8,128)(2,1)S(1)} %fusion.61), channel_id=1, source_target_pairs={{0,32},{8,40},{16,48},{24,56},{32,0},{40,8},{48,16},{56,24},{64,96... | collective-permute-start | bytes 786440 | tf_op jit(solution)/shard_map/ppermute | solution.py:11
  156.5 23.2 %collective-permute-start.7 = (bf16[8,3,128,128]{3,2,1,0:T(8,128)(2,1)S(1)}, bf16[8,3,128,128]{3,2,1,0:T(8,128)(2,1)S(1)}, u32[]{:S(2)}, u32[]{:S(2)}) collective-permute-start(bf16[8,3,128,128]{3,2,1,0:T(8,128)(2,1)S(1)} %pad_maximum_fusion.2), channel_id=1, source_target_pairs={{0,32},{8,40},{16,48},{24,56},{32,0},{40,8},{48,16},{56,24},{64,96... | collective-permute-start | bytes 2359304 | tf_op jit(solution)/shard_map/ppermute | solution.py:11
  164.6 7.0 %collective-permute-start.3 = (bf16[8,128,128]{2,1,0:T(8,128)(2,1)S(1)}, bf16[8,128,128]{2,1,0:T(8,128)(2,1)S(1)}, u32[]{:S(2)}, u32[]{:S(2)}) collective-permute-start(bf16[8,128,128]{2,1,0:T(8,128)(2,1)S(1)} %fusion.42), channel_id=1, source_target_pairs={{0,64},{8,72},{16,80},{24,88},{32,96},{40,104},{48,112},{56,120},{... | collective-permute-start | bytes 786440 | tf_op jit(solution)/shard_map/ppermute | solution.py:11
  171.8 8.8 %collective-permute-start.4 = (bf16[8,128,128]{2,1,0:T(8,128)(2,1)S(1)}, bf16[8,128,128]{2,1,0:T(8,128)(2,1)S(1)}, u32[]{:S(2)}, u32[]{:S(2)}) collective-permute-start(bf16[8,128,128]{2,1,0:T(8,128)(2,1)S(1)} %add_convert_fusion), channel_id=1, source_target_pairs={{0,128},{8,136},{16,144},{24,152},{32,160},{40,168},{48,176},{56,1... | collective-permute-start | bytes 786440 | tf_op jit(solution)/shard_map/ppermute | solution.py:11
  180.2 12.4 %collective-permute-start.8 = (bf16[8,2,128,128]{3,2,1,0:T(8,128)(2,1)S(1)}, bf16[8,2,128,128]{3,2,1,0:T(8,128)(2,1)S(1)}, u32[]{:S(2)}, u32[]{:S(2)}) collective-permute-start(bf16[8,2,128,128]{3,2,1,0:T(8,128)(2,1)S(1)} %pad_maximum_fusion.3), channel_id=1, source_target_pairs={{0,64},{8,72},{16,80},{24,88},{32,96},{40,104},{48,112},{56,120},{... | collective-permute-start | bytes 1572872 | tf_op jit(solution)/shard_map/ppermute | solution.py:11
  180.6 15.1 %copy-start.5 = (bf16[8,128,5,128]{3,1,0,2:T(8,128)(2,1)}, bf16[8,128,5,128]{3,1,0,2:T(8,128)(2,1)S(1)}, u32[]{:S(2)}) copy-start(bf16[8,128,5,128]{3,1,0,2:T(8,128)(2,1)S(1)} %bitcast_dynamic-update-slice_fusion) | copy-start | bytes 3932164
  192.9 8.0 %collective-permute-start.9 = (bf16[8,1,128,128]{3,2,1,0:T(8,128)(2,1)S(1)}, bf16[8,1,128,128]{3,2,1,0:T(8,128)(2,1)S(1)}, u32[]{:S(2)}, u32[]{:S(2)}) collective-permute-start(bf16[8,1,128,128]{3,2,1,0:T(8,128)(2,1)S(1)} %fusion.21), channel_id=1, source_target_pairs={{0,128},{8,136},{16,144},{24,152},{32,160},{40,168},{48,176},{56,1... | collective-permute-start | bytes 786440 | tf_op jit(solution)/shard_map/ppermute | solution.py:11
  224.9 186.6 %all-reduce.2.cloned.1.call-start = ((), (), s32[]{:S(2)}) async-start(), calls=%async_computation.3 | async-start | bytes 786432 | tf_op jit(solution)/shard_map/psum | solution.py:126
  336.3 2.4 copy-start.3
Sparse Core Ops, SparseCore 0:
  10.6 70.8 all-gather.1
  225.0 111.1 reduce-scatter.1
  338.7 72.7 all-reduce.1
where the time goes:
time: 421 us; the launch traced here: 420 us
  waiting for transfers between devices  319 us (76%)
  local copies, waits for them, and re-layouts  42.8 us (10%)
  matrix products  26 us (6%)
  between operations  14.1 us (3%)
  starting transfers between devices  10.3 us (2%)
  other arithmetic  7.66 us (2%)
    reduce_scatter x1, waiting for transfers between devices, per_device(): lax.psum_scatter(partial_value.reshape(lax.axis_size('seq') * shard_rows,...  111 us
    psum x1, waiting for transfers between devices, per_device(): grad_w = lax.psum(seq_sum, 'dp').astype(jnp.float32)  71.2 us
    all_gather x1, waiting for transfers between devices, per_device(): lax.all_gather(w_qkv, 'seq', axis=0, tiled=True)  71.2 us
    ppermute x10, waiting for transfers between devices, swapped(): return lax.ppermute(value, axis, pairs)  64.7 us
    all_gather x1, local copies, waits for them, and re-layouts, per_device(): lax.all_gather(w_qkv, 'seq', axis=0, tiled=True)  17 us
    convert_element_type x1, local copies, waits for them, and re-layouts, per_device(): partial_value.reshape(lax.axis_size('seq') * shard_rows, 3, inner_width)  16.6 us
    ppermute x10, starting transfers between devices, swapped(): return lax.ppermute(value, axis, pairs)  10.1 us
  transfers between devices with their start and end apart: 13, of which 9 were waited for; matrix products, arithmetic and copies ran while one was open for 4% of the time, Pallas kernels for 0%

commit v1 on v0

--- a/solution.py
+++ b/solution.py
@@ -62,7 +62,11 @@
     levels = lax.axis_size("seq").bit_length() - 1
     device = lax.axis_index("seq")
     projected = make_adder(
-        inputs, 3 * inner_width, lax.all_gather(w_qkv, "seq", axis=0, tiled=True)
+        inputs,
+        3 * inner_width,
+        jnp.concatenate(
+            lax.all_to_all(jnp.stack([w_qkv] * lax.axis_size("seq")), "seq", 0, 0), axis=0
+        ),
     )
     projected = projected.astype(jnp.bfloat16).reshape(block_len, 3, head_count, head_dim)
     queries = projected[:, 0]

time: 421 us -> 534 us (1.27)
  waiting for transfers between devices: 319 us -> 399 us
  local copies, waits for them, and re-layouts: 42.8 us -> 60.1 us
  starting transfers between devices: 10.3 us -> 25.5 us
    all_to_all x0 -> x1, waiting for transfers between devices: none -> 149 us  [per_device(): lax.all_to_all(jnp.stack([w_qkv] * lax.axis_size('seq')), 'seq', 0, 0)]
    all_gather x1 -> x0, waiting for transfers between devices: 71.2 us -> none  [per_device(): lax.all_gather(w_qkv, 'seq', axis=0, tiled=True)]
    all_gather x1 -> x0, local copies, waits for them, and re-layouts: 17 us -> none  [per_device(): lax.all_gather(w_qkv, 'seq', axis=0, tiled=True)]
    all_to_all x0 -> x1, local copies, waits for them, and re-layouts: none -> 16.7 us  [per_device(): lax.all_to_all(jnp.stack([w_qkv] * lax.axis_size('seq')), 'seq', 0, 0)]
    unnamed x20 -> x27, local copies, waits for them, and re-layouts: 4.3 us -> 14.7 us
    all_to_all x0 -> x1, starting transfers between devices: none -> 7.8 us  [per_device(): lax.all_to_all(jnp.stack([w_qkv] * lax.axis_size('seq')), 'seq', 0, 0)]
    ppermute x10, starting transfers between devices: 10.1 us -> 17.6 us  [swapped(): return lax.ppermute(value, axis, pairs)]
    another operation x0 -> x1, local copies, waits for them, and re-layouts: none -> 7.19 us  [per_device(): jnp.stack([w_qkv] * lax.axis_size('seq'))]
  transfers between devices with their start and end apart: 13 -> 13, of which waited for: 9 -> 10; matrix products, arithmetic and copies ran while one was open for 4% -> 3% of each run, Pallas kernels for 0% -> 0%
where the time goes in v1:
time: 534 us; the launch traced here: 533 us
  waiting for transfers between devices  399 us (75%)
  local copies, waits for them, and re-layouts  60.1 us (11%)
  matrix products  26.4 us (5%)
  starting transfers between devices  25.5 us (5%)
  between operations  14.5 us (3%)
  other arithmetic  7.67 us (1%)
    all_to_all x1, waiting for transfers between devices, per_device(): lax.all_to_all(jnp.stack([w_qkv] * lax.axis_size('seq')), 'seq', 0, 0)  149 us
    reduce_scatter x1, waiting for transfers between devices, per_device(): lax.psum_scatter(partial_value.reshape(lax.axis_size('seq') * shard_rows,...  112 us
    psum x1, waiting for transfers between devices, per_device(): grad_w = lax.psum(seq_sum, 'dp').astype(jnp.float32)  71.2 us
    ppermute x10, waiting for transfers between devices, swapped(): return lax.ppermute(value, axis, pairs)  67.3 us
    ppermute x10, starting transfers between devices, swapped(): return lax.ppermute(value, axis, pairs)  17.6 us
    all_to_all x1, local copies, waits for them, and re-layouts, per_device(): lax.all_to_all(jnp.stack([w_qkv] * lax.axis_size('seq')), 'seq', 0, 0)  16.7 us
    convert_element_type x1, local copies, waits for them, and re-layouts, per_device(): partial_value.reshape(lax.axis_size('seq') * shard_rows, 3, inner_width)  16.6 us
    unnamed x27, local copies, waits for them, and re-layouts  14.7 us
  transfers between devices with their start and end apart: 13, of which 10 were waited for; matrix products, arithmetic and copies ran while one was open for 3% of the time, Pallas kernels for 0%

profile of v1, /device:TPU:2, one launch (start us, length us, event | category | flops | bytes accessed | tf_op | source)
XLA Modules:
  0.0 532.8 jit_solution(17896873544786677937)
XLA Ops:
  7.2 7.2 %stack.42 = bf16[32,64,3,1024]{3,1,2,0:T(8,128)(2,1)} broadcast(bf16[64,3,1024]{2,0,1:T(8,128)(2,1)} %param.6), dimensions={1,2,3} | broadcast | bytes 12976128 | tf_op jit(solution)/shard_map/stack | solution.py:68
  14.4 7.8 %all-to-all-start = ((bf16[32,64,3,1024]{3,1,2,0:T(8,128)(2,1)}), bf16[32,64,3,1024]{3,1,2,0:T(8,128)(2,1)}, u32[]{:S(2)}, u32[]{:S(2)}) async-start(bf16[32,64,3,1024]{3,1,2,0:T(8,128)(2,1)} %stack.42), calls=%async_computation | async-start | bytes 25165824 | tf_op jit(solution)/shard_map/all_to_all | solution.py:68
  22.9 148.7 %all-to-all-done = bf16[32,64,3,1024]{3,1,2,0:T(8,128)(2,1)} async-done(((bf16[32,64,3,1024]{3,1,2,0:T(8,128)(2,1)}), bf16[32,64,3,1024]{3,1,2,0:T(8,128)(2,1)}, u32[]{:S(2)}, u32[]{:S(2)}) %all-to-all-start) | async-done | bytes 12582944 | tf_op jit(solution)/shard_map/all_to_all | solution.py:68
  171.6 16.7 %copy.53 = bf16[32,64,3,1024]{3,2,1,0:T(4,128)(2,1)S(1)} copy(bf16[32,64,3,1024]{3,1,2,0:T(8,128)(2,1)} %all-to-all-done) | data formatting | bytes 25165824 | tf_op jit(solution)/shard_map/all_to_all | solution.py:68
  188.4 11.4 %copy.96 = bf16[256,8,3,1024]{3,1,2,0:T(8,128)(2,1)} copy(bf16[256,8,3,1024]{3,2,1,0:T(4,128)(2,1)S(1)} %bitcast.132) | data formatting | bytes 25165824
  199.8 8.0 %fusion.6 = bf16[32,8,24,128]{3,1,2,0:T(8,128)(2,1)S(1)} fusion(bf16[2048,3072]{1,0:T(8,128)(2,1)} %bitcast.134, bf16[1,256,2048]{2,1,0:T(8,128)(2,1)S(1)} %copy-done), kind=kOutput, calls=%fused_computation.14 | convolution fusion | flops 3222011904 | bytes 15204352 | tf_op jit(solution)/shard_map/dot_general | solution.py:30
  210.3 2.5 copy.69
  212.8 3.9 fusion.67
  222.3 1.8 convert_element_type.144
  224.9 11.8 %collective-permute-start.6 = (bf16[8,4,128,128]{3,2,1,0:T(8,128)(2,1)S(1)}, bf16[8,4,128,128]{3,2,1,0:T(8,128)(2,1)S(1)}, u32[]{:S(2)}, u32[]{:S(2)}) collective-permute-start(bf16[8,4,128,128]{3,2,1,0:T(8,128)(2,1)S(1)} %pad_maximum_fusion.1), channel_id=1, source_target_pairs={{0,16},{8,24},{16,0},{24,8},{32,48},{40,56},{48,32},{56,40},{64,80... | collective-permute-start | bytes 3145736 | tf_op jit(solution)/shard_map/ppermute | solution.py:11
  237.7 28.0 %collective-permute-done.1 = bf16[8,128,128]{2,1,0:T(8,128)(2,1)S(1)} collective-permute-done((bf16[8,128,128]{2,1,0:T(8,128)(2,1)S(1)}, bf16[8,128,128]{2,1,0:T(8,128)(2,1)S(1)}, u32[]{:S(2)}, u32[]{:S(2)}) %collective-permute-start.1) | collective-permute-done | bytes 262176 | tf_op jit(solution)/shard_map/ppermute | solution.py:11
  266.5 3.6 collective-permute-start.7
  270.1 6.4 %collective-permute-done.2 = bf16[8,128,128]{2,1,0:T(8,128)(2,1)S(1)} collective-permute-done((bf16[8,128,128]{2,1,0:T(8,128)(2,1)S(1)}, bf16[8,128,128]{2,1,0:T(8,128)(2,1)S(1)}, u32[]{:S(2)}, u32[]{:S(2)}) %collective-permute-start.2) | collective-permute-done | bytes 262176 | tf_op jit(solution)/shard_map/ppermute | solution.py:11
  276.9 8.8 %collective-permute-done.3 = bf16[8,128,128]{2,1,0:T(8,128)(2,1)S(1)} collective-permute-done((bf16[8,128,128]{2,1,0:T(8,128)(2,1)S(1)}, bf16[8,128,128]{2,1,0:T(8,128)(2,1)S(1)}, u32[]{:S(2)}, u32[]{:S(2)}) %collective-permute-start.3) | collective-permute-done | bytes 262176 | tf_op jit(solution)/shard_map/ppermute | solution.py:11
  285.9 5.9 %collective-permute-done.7 = bf16[8,3,128,128]{3,2,1,0:T(8,128)(2,1)S(1)} collective-permute-done((bf16[8,3,128,128]{3,2,1,0:T(8,128)(2,1)S(1)}, bf16[8,3,128,128]{3,2,1,0:T(8,128)(2,1)S(1)}, u32[]{:S(2)}, u32[]{:S(2)}) %collective-permute-start.7) | collective-permute-done | bytes 786464 | tf_op jit(solution)/shard_map/ppermute | solution.py:11
  292.6 2.4 collective-permute-done.4
  295.0 9.9 %collective-permute-done.8 = bf16[8,2,128,128]{3,2,1,0:T(8,128)(2,1)S(1)} collective-permute-done((bf16[8,2,128,128]{3,2,1,0:T(8,128)(2,1)S(1)}, bf16[8,2,128,128]{3,2,1,0:T(8,128)(2,1)S(1)}, u32[]{:S(2)}, u32[]{:S(2)}) %collective-permute-start.8) | collective-permute-done | bytes 524320 | tf_op jit(solution)/shard_map/ppermute | solution.py:11
  307.4 5.9 %collective-permute-done.9 = bf16[8,1,128,128]{3,2,1,0:T(8,128)(2,1)S(1)} collective-permute-done((bf16[8,1,128,128]{3,2,1,0:T(8,128)(2,1)S(1)}, bf16[8,1,128,128]{3,2,1,0:T(8,128)(2,1)S(1)}, u32[]{:S(2)}, u32[]{:S(2)}) %collective-permute-start.9) | collective-permute-done | bytes 262176 | tf_op jit(solution)/shard_map/ppermute | solution.py:11
  314.3 6.3 %convolution_convert_fusion = bf16[3072,2048]{1,0:T(8,128)(2,1)} fusion(bf16[256,3072]{0,1:T(8,128)(2,1)S(1)} %bitcast.135, bf16[1,256,2048]{2,1,0:T(8,128)(2,1)S(1)} %copy-done), kind=kOutput, calls=%fused_computation | convolution fusion | flops 3227516928 | bytes 15204352 | tf_op jit(solution)/shard_map/tr,tc->rc/dot_general | solution.py:121
  320.6 16.6 %copy.74 = bf16[2048,3,1024]{2,0,1:T(8,128)(2,1)} copy(bf16[2048,3,1024]{0,2,1:T(8,128)(2,1)} %bitcast.133) | data formatting | bytes 25165824 | tf_op jit(solution)/shard_map/convert_element_type | solution.py:123
  337.3 111.6 %reduce-scatter.2.cloned.1.call-done = bf16[64,3,1024]{2,0,1:T(8,128)(2,1)} async-done(((bf16[2048,3,1024]{2,0,1:T(8,128)(2,1)}), bf16[64,3,1024]{2,0,1:T(8,128)(2,1)}) %reduce-scatter.2.cloned.1.call-update) | async-done | bytes 393232 | tf_op jit(solution)/shard_map/reduce_scatter | solution.py:122
  448.9 2.4 fusion.1
  452.9 71.2 %all-reduce.2.cloned.1.call-done = bf16[64,3,1024]{2,0,1:T(8,128)(2,1)} async-done(((bf16[64,3,1024]{2,0,1:T(8,128)(2,1)}), bf16[64,3,1024]{2,0,1:T(8,128)(2,1)}) %all-reduce.2.cloned.1.call-update) | async-done | bytes 393232 | tf_op jit(solution)/shard_map/psum | solution.py:130
  524.0 2.0 convert_element_type.159
  (79 shorter events, 17.6 us)
Async XLA Ops:
  7.2 192.7 %copy-start = (bf16[1,256,2048]{2,1,0:T(8,128)(2,1)S(1)}, bf16[1,256,2048]{2,1,0:T(8,128)(2,1)}, u32[]{:S(2)}) copy-start(bf16[1,256,2048]{2,1,0:T(8,128)(2,1)} %param.5) | copy-start | bytes 3145732
  14.4 7.9 %copy-start.7 = (f32[16,8]{0,1:T(8,128)S(1)}, f32[16,8]{0,1:T(8,128)}, u32[]{:S(2)}) copy-start(f32[16,8]{0,1:T(8,128)} %param.7) | copy-start | bytes 1540
  14.4 7.9 %copy-start.8 = (s32[1,2,6]{2,1,0:T(2,128)S(1)}, s32[1,2,6]{2,1,0:T(2,128)}, u32[]{:S(2)}) copy-start(s32[1,2,6]{2,1,0:T(2,128)} %param.8) | copy-start | bytes 148
  14.4 8.4 %copy-start.5 = (bf16[1,256,1024]{2,1,0:T(8,128)(2,1)S(1)}, bf16[1,256,1024]{2,1,0:T(8,128)(2,1)}, u32[]{:S(2)}) copy-start(bf16[1,256,1024]{2,1,0:T(8,128)(2,1)} %param.9) | copy-start | bytes 1572868
  14.4 157.3 %all-to-all-start = ((bf16[32,64,3,1024]{3,1,2,0:T(8,128)(2,1)}), bf16[32,64,3,1024]{3,1,2,0:T(8,128)(2,1)}, u32[]{:S(2)}, u32[]{:S(2)}) async-start(bf16[32,64,3,1024]{3,1,2,0:T(8,128)(2,1)} %stack.42), calls=%async_computation | async-start | bytes 25165824 | tf_op jit(solution)/shard_map/all_to_all | solution.py:68
  22.2 426.7 %reduce-scatter.2.cloned.1.call-start = ((), (), s32[]{:S(2)}) async-start(), calls=%async_computation.2 | async-start | bytes 12976128 | tf_op jit(solution)/shard_map/reduce_scatter | solution.py:122
  216.8 5.5 %collective-permute-start.5 = (bf16[8,5,128,128]{3,2,1,0:T(8,128)(2,1)}, bf16[8,5,128,128]{3,2,1,0:T(8,128)(2,1)}, u32[]{:S(2)}, u32[]{:S(2)}) collective-permute-start(bf16[8,5,128,128]{3,2,1,0:T(8,128)(2,1)} %get-tuple-element.23), channel_id=1, source_target_pairs={{0,8},{8,0},{16,24},{24,16},{32,40},{40,32},{48,56},{56,48},{64,72... | collective-permute-start | bytes 3932168 | tf_op jit(solution)/shard_map/ppermute | solution.py:11
  219.6 17.6 %collective-permute-start = (bf16[8,128,128]{2,1,0:T(8,128)(2,1)S(1)}, bf16[8,128,128]{2,1,0:T(8,128)(2,1)S(1)}, u32[]{:S(2)}, u32[]{:S(2)}) collective-permute-start(bf16[8,128,128]{2,1,0:T(8,128)(2,1)S(1)} %get-tuple-element.21), channel_id=1, source_target_pairs={{0,8},{8,0},{16,24},{24,16},{32,40},{40,32},{48,56},{56,48},{64,72... | collective-permute-start | bytes 786440 | tf_op jit(solution)/shard_map/ppermute | solution.py:11
  222.3 2.1 copy-start.1
  224.9 12.5 %copy-start.4 = (bf16[256,8,128]{0,2,1:T(8,128)(2,1)S(1)}, bf16[256,8,128]{0,2,1:T(8,128)(2,1)}, u32[]{:S(2)}) copy-start(bf16[256,8,128]{0,2,1:T(8,128)(2,1)} %copy.72) | copy-start | bytes 1572868
  224.9 40.9 %collective-permute-start.6 = (bf16[8,4,128,128]{3,2,1,0:T(8,128)(2,1)S(1)}, bf16[8,4,128,128]{3,2,1,0:T(8,128)(2,1)S(1)}, u32[]{:S(2)}, u32[]{:S(2)}) collective-permute-start(bf16[8,4,128,128]{3,2,1,0:T(8,128)(2,1)S(1)} %pad_maximum_fusion.1), channel_id=1, source_target_pairs={{0,16},{8,24},{16,0},{24,8},{32,48},{40,56},{48,32},{56,40},{64,80... | collective-permute-start | bytes 3145736 | tf_op jit(solution)/shard_map/ppermute | solution.py:11
  237.2 28.6 %copy-start.2 = (bf16[8,256,256]{2,1,0:T(8,128)(2,1)}, bf16[8,256,256]{2,1,0:T(8,128)(2,1)S(1)}, u32[]{:S(2)}) copy-start(bf16[8,256,256]{2,1,0:T(8,128)(2,1)S(1)} %select_convert_fusion) | copy-start | bytes 3145732
  237.2 28.4 %collective-permute-start.1 = (bf16[8,128,128]{2,1,0:T(8,128)(2,1)S(1)}, bf16[8,128,128]{2,1,0:T(8,128)(2,1)S(1)}, u32[]{:S(2)}, u32[]{:S(2)}) collective-permute-start(bf16[8,128,128]{2,1,0:T(8,128)(2,1)S(1)} %fusion.41), channel_id=1, source_target_pairs={{0,16},{8,24},{16,0},{24,8},{32,48},{40,56},{48,32},{56,40},{64,80... | collective-permute-start | bytes 786440 | tf_op jit(solution)/shard_map/ppermute | solution.py:11
  265.7 10.8 %collective-permute-start.2 = (bf16[8,128,128]{2,1,0:T(8,128)(2,1)S(1)}, bf16[8,128,128]{2,1,0:T(8,128)(2,1)S(1)}, u32[]{:S(2)}, u32[]{:S(2)}) collective-permute-start(bf16[8,128,128]{2,1,0:T(8,128)(2,1)S(1)} %fusion.61), channel_id=1, source_target_pairs={{0,32},{8,40},{16,48},{24,56},{32,0},{40,8},{48,16},{56,24},{64,96... | collective-permute-start | bytes 786440 | tf_op jit(solution)/shard_map/ppermute | solution.py:11
  266.5 25.4 %collective-permute-start.7 = (bf16[8,3,128,128]{3,2,1,0:T(8,128)(2,1)S(1)}, bf16[8,3,128,128]{3,2,1,0:T(8,128)(2,1)S(1)}, u32[]{:S(2)}, u32[]{:S(2)}) collective-permute-start(bf16[8,3,128,128]{3,2,1,0:T(8,128)(2,1)S(1)} %pad_maximum_fusion.2), channel_id=1, source_target_pairs={{0,32},{8,40},{16,48},{24,56},{32,0},{40,8},{48,16},{56,24},{64,96... | collective-permute-start | bytes 2359304 | tf_op jit(solution)/shard_map/ppermute | solution.py:11
  276.7 9.0 %collective-permute-start.3 = (bf16[8,128,128]{2,1,0:T(8,128)(2,1)S(1)}, bf16[8,128,128]{2,1,0:T(8,128)(2,1)S(1)}, u32[]{:S(2)}, u32[]{:S(2)}) collective-permute-start(bf16[8,128,128]{2,1,0:T(8,128)(2,1)S(1)} %fusion.42), channel_id=1, source_target_pairs={{0,64},{8,72},{16,80},{24,88},{32,96},{40,104},{48,112},{56,120},{... | collective-permute-start | bytes 786440 | tf_op jit(solution)/shard_map/ppermute | solution.py:11
  285.8 9.1 %collective-permute-start.4 = (bf16[8,128,128]{2,1,0:T(8,128)(2,1)S(1)}, bf16[8,128,128]{2,1,0:T(8,128)(2,1)S(1)}, u32[]{:S(2)}, u32[]{:S(2)}) collective-permute-start(bf16[8,128,128]{2,1,0:T(8,128)(2,1)S(1)} %add_convert_fusion), channel_id=1, source_target_pairs={{0,128},{8,136},{16,144},{24,152},{32,160},{40,168},{48,176},{56,1... | collective-permute-start | bytes 786440 | tf_op jit(solution)/shard_map/ppermute | solution.py:11
  292.4 12.5 %collective-permute-start.8 = (bf16[8,2,128,128]{3,2,1,0:T(8,128)(2,1)S(1)}, bf16[8,2,128,128]{3,2,1,0:T(8,128)(2,1)S(1)}, u32[]{:S(2)}, u32[]{:S(2)}) collective-permute-start(bf16[8,2,128,128]{3,2,1,0:T(8,128)(2,1)S(1)} %pad_maximum_fusion.3), channel_id=1, source_target_pairs={{0,64},{8,72},{16,80},{24,88},{32,96},{40,104},{48,112},{56,120},{... | collective-permute-start | bytes 1572872 | tf_op jit(solution)/shard_map/ppermute | solution.py:11
  295.0 12.0 %copy-start.6 = (bf16[8,128,5,128]{3,1,0,2:T(8,128)(2,1)}, bf16[8,128,5,128]{3,1,0,2:T(8,128)(2,1)S(1)}, u32[]{:S(2)}) copy-start(bf16[8,128,5,128]{3,1,0,2:T(8,128)(2,1)S(1)} %bitcast_dynamic-update-slice_fusion) | copy-start | bytes 3932164
  305.1 8.2 %collective-permute-start.9 = (bf16[8,1,128,128]{3,2,1,0:T(8,128)(2,1)S(1)}, bf16[8,1,128,128]{3,2,1,0:T(8,128)(2,1)S(1)}, u32[]{:S(2)}, u32[]{:S(2)}) collective-permute-start(bf16[8,1,128,128]{3,2,1,0:T(8,128)(2,1)S(1)} %fusion.21), channel_id=1, source_target_pairs={{0,128},{8,136},{16,144},{24,152},{32,160},{40,168},{48,176},{56,1... | collective-permute-start | bytes 786440 | tf_op jit(solution)/shard_map/ppermute | solution.py:11
  337.3 186.7 %all-reduce.2.cloned.1.call-start = ((), (), s32[]{:S(2)}) async-start(), calls=%async_computation.3 | async-start | bytes 786432 | tf_op jit(solution)/shard_map/psum | solution.py:130
  448.9 2.4 copy-start.3
Sparse Core Ops, SparseCore 0:
  337.4 111.4 reduce-scatter.1
  451.3 72.6 all-reduce.1
